TPU v7x, 128 devices: a whole 4x4x4 slice. The times are simulated.
128 devices in a mesh: site: 32 (over z, x, core), band: 4 (over y).
Axes of the slice: x: 4, y: 4, z: 4, core: 2. Of those that a mesh axis runs over, the one named last changes fastest.
Arguments:
- fields: bfloat16 [4096, 32, 4096], P('site', None, 'band'), may hold values from -6 to 6
- factor: bfloat16 [4096, 4, 128], P('site'), may hold values from -0.25 to 0.25
- pattern: int32 [32, 3], P('site'), may hold values 0 or 1
- tx_power: float32 [4096], replicated, may hold values from 30 to 49
- site_position: float32 [2, 4096], replicated, may hold values from 0 to 1, as said below
- candidates: int32 [32, 16], P('site'), may hold values from 0 to 4095, as said below
Outputs:
- best_level: float32 [32, 4096], P('site', 'band')
- sinr_level: float32 [32, 4096], P('site', 'band')
- tile_mean: float32 [32], P('site')
Inputs may be any that keep to these rules, and one draw needn't show every extreme that they name: `site_position`: tile t covers column t % 8 and row t // 8 of a grid of 8 x (4) tiles over the window. Site s lies in tile s // 128, which is cut into 16 columns by 8 rows of equal cells, each holding exactly one of the tile's sites. The candidates of tile t are its 16 sites in the top row of cells, in order of cell column; they are distinct.
All inputs are finite; a program needn't handle non-finite values. No bound on the sum of `pattern` on one device may be relied on, other than what follows from the above.
Results may differ from a plain program's by a relative error of at most 0.005.
Values may be sent and summed in bfloat16 or wider, within the bound.
A program may use at most 192 MiB of HBM per device.

v0:
```python
import jax
import jax.numpy as jnp
from jax import lax
from jax.sharding import PartitionSpec as P

COLS = 256


spacing = 0.03
ln_tenth = 0.2302585093


def shifted(block, axis, distance):
    devices = range(lax.axis_size(axis))
    route = [(i - distance, i) for i in devices if i - distance in devices]
    return lax.ppermute(block, axis, route)


def coverage(mixed, tile_number, row_start, row_count, height, tx_power, site_position, cand_row):
    pixel = jnp.arange(row_count * COLS, dtype=jnp.int32)
    row_index = row_start + pixel // COLS
    col_index = pixel % COLS
    pos_x = (tile_number % 8 * COLS + col_index).astype(jnp.float32) * spacing
    pos_y = (tile_number // 8 * COLS + row_index).astype(jnp.float32) * spacing
    site_x = site_position[0] * (8.0 * COLS * spacing)
    site_y = site_position[1] * (height * COLS * spacing)
    dist = jnp.sqrt(
        (site_x[:, None] - pos_x[None, :]) ** 2
        + (site_y[:, None] - pos_y[None, :]) ** 2
        + spacing * spacing
    )
    level = (
        tx_power[:, None]
        - (100.0 + 22.0 * jnp.log10(dist))
        + 8.0 * mixed.astype(jnp.float32)
        + 90.0
    )
    power = jnp.exp(ln_tenth * level)
    cand_power = jnp.take(power, cand_row, axis=0)
    best = jnp.max(cand_power, axis=0)
    serving = jnp.take(cand_row, jnp.argmax(cand_power, axis=0))
    site_ids = jnp.arange(power.shape[0], dtype=jnp.int32)
    interference = jnp.sum(jnp.where(site_ids[:, None] == serving[None, :], 0.0, power), axis=0)
    return (jnp.log10(best), jnp.log10(best / interference))


def shards(fields, factor, pattern, tx_power, site_position, candidates):
    block = fields.shape[0]
    depth = factor.shape[1]
    lower = jnp.tril(jnp.ones((block, block), jnp.bfloat16))
    total = jnp.einsum(
        "ik,ktp->itp", factor[:, 0, :] * lower, fields, preferred_element_type=jnp.float32
    )
    for offset in range(1, depth):
        earlier = shifted(fields, "site", offset)
        weights = factor[:, offset, :] * pattern[0, offset - 1].astype(jnp.bfloat16)
        total = total + jnp.einsum(
            "ik,ktp->itp", weights, earlier, preferred_element_type=jnp.float32
        )
    mixed = lax.all_to_all(
        total.astype(jnp.bfloat16), "site", split_axis=1, concat_axis=0, tiled=True
    )
    tiles_here = mixed.shape[1]
    row_count = mixed.shape[2] // COLS
    band_start = lax.axis_index("band") * row_count
    first_tile = lax.axis_index("site") * tiles_here
    height = lax.axis_size("site") * tiles_here // 8
    best_part, sinr_part = coverage(
        mixed[:, 0, :],
        first_tile + 0,
        band_start,
        row_count,
        height,
        tx_power,
        site_position,
        candidates[0],
    )
    best_rows = [best_part]
    sinr_rows = [sinr_part]
    best_level = jnp.stack(best_rows, axis=0)
    sinr_level = jnp.stack(sinr_rows, axis=0)
    share = jnp.sum(sinr_level, axis=1) / float(row_count * COLS * lax.axis_size("band"))
    tile_mean = lax.psum(share, "band")
    return (best_level, sinr_level, tile_mean)


def solution(mesh):
    placed = (
        P("site", None, "band"),
        P("site", None, None),
        P("site", None),
        P(),
        P(),
        P("site", None),
    )
    return jax.shard_map(
        shards,
        mesh=mesh,
        in_specs=placed,
        out_specs=(P("site", "band"), P("site", "band"), P("site")),
        check_vma=False,
    )
```

profile of v0, /device:TPU:102, one launch (start us, length us, event | category | flops | bytes accessed | tf_op | source)
XLA Modules:
  0.0 664.5 jit_solution(4354762217575115813)
XLA Ops:
  0.7 11.3 %copy.17 = bf16[128,32,1024]{2,0,1:T(8,128)(2,1)} copy(bf16[128,32,1024]{2,1,0:T(8,128)(2,1)} %param.6) | data formatting | bytes 16777216 | tf_op args[0]
  12.0 1.3 collective-permute-start.1
  13.3 1.9 collective-permute-start
  15.2 1.5 collective-permute-start.2
  16.7 0.6 fusion.48
  17.3 0.2 fusion.46
  17.5 19.7 %fusion.11 = f32[128,32,1024]{2,0,1:T(8,128)} fusion(bf16[128,1,128]{2,1,0:T(2,128)(2,1)S(1)} %get-tuple-element.13, bf16[128,32,1024]{2,1,0:T(8,128)(2,1)} %param.6), kind=kOutput, calls=%fused_computation.18 | convolution fusion | flops 1073840128 | bytes 25198592 | tf_op jit(solution)/shard_map/ik,ktp->itp/dot_general | solution.py:51
  37.2 160.2 %collective-permute-done.1 = bf16[128,32,1024]{2,0,1:T(8,128)(2,1)S(1)} collective-permute-done((bf16[128,32,1024]{2,0,1:T(8,128)(2,1)}, bf16[128,32,1024]{2,0,1:T(8,128)(2,1)S(1)}, u32[]{:S(2)}, u32[]{:S(2)}) %collective-permute-start.1) | collective-permute-done | bytes 8388640 | tf_op jit(solution)/shard_map/ppermute | solution.py:16
  197.4 8.9 %fusion.19 = f32[128,32,1024]{2,0,1:T(8,128)} fusion(bf16[128,32,1024]{2,0,1:T(8,128)(2,1)S(1)} %collective-permute-done.1, bf16[128,1,128]{2,1,0:T(2,128)(2,1)S(1)} %get-tuple-element.11, bf16[]{:T(256)} %bitcast.8), kind=kOutput, calls=%fused_computation.24 | convolution fusion | flops 1073807360 | bytes 25198594 | tf_op jit(solution)/shard_map/ik,ktp->itp/dot_general | solution.py:57
  206.3 168.5 %collective-permute-done = bf16[128,32,1024]{2,0,1:T(8,128)(2,1)S(1)} collective-permute-done((bf16[128,32,1024]{2,0,1:T(8,128)(2,1)}, bf16[128,32,1024]{2,0,1:T(8,128)(2,1)S(1)}, u32[]{:S(2)}, u32[]{:S(2)}) %collective-permute-start) | collective-permute-done | bytes 8388640 | tf_op jit(solution)/shard_map/ppermute | solution.py:16
  374.9 8.7 %fusion.22 = f32[128,32,1024]{2,0,1:T(8,128)} fusion(bf16[128,32,1024]{2,0,1:T(8,128)(2,1)S(1)} %collective-permute-done, bf16[128,1,128]{2,1,0:T(2,128)(2,1)S(1)} %get-tuple-element.12, bf16[]{:T(256)} %bitcast.5), kind=kOutput, calls=%fused_computation.27 | convolution fusion | flops 1073807360 | bytes 25198594 | tf_op jit(solution)/shard_map/ik,ktp->itp/dot_general | solution.py:57
  383.6 23.6 %add_convert_fusion = bf16[128,32,1024]{2,0,1:T(8,128)(2,1)} fusion(f32[128,32,1024]{2,0,1:T(8,128)} %fusion.19, f32[128,32,1024]{2,0,1:T(8,128)} %fusion.11, f32[128,32,1024]{2,0,1:T(8,128)} %fusion.22, bf16[128,32,1024]{2,0,1:T(8,128)(2,1)} %collective-permute-done.2, bf16[128,1,128]{2,1,0:T(2,128)(2,1)S(1)} %get-tuple-element.10, bf16[]{:T(256)} %bitcast.11), kind=kOutput, calls=%fused_computation.12 | convolution fusion | flops 1090584576 | bytes 67141632 | tf_op jit(solution)/shard_map/ik,ktp->itp/dot_general | solution.py:57
  407.2 89.8 %all-to-all-start = ((bf16[128,32,1024]{2,0,1:T(8,128)(2,1)}), bf16[128,32,1024]{2,0,1:T(8,128)(2,1)}, u32[]{:S(2)}, u32[]{:S(2)}) async-start(bf16[128,32,1024]{2,0,1:T(8,128)(2,1)} %add_convert_fusion), calls=%async_computation | async-start | bytes 16777216 | tf_op jit(solution)/shard_map/all_to_all | solution.py:60
  497.0 0.0 copy-start.3
  497.1 0.7 fusion.47
  497.9 94.9 %all-to-all-done = bf16[128,32,1024]{2,0,1:T(8,128)(2,1)} async-done(((bf16[128,32,1024]{2,0,1:T(8,128)(2,1)}), bf16[128,32,1024]{2,0,1:T(8,128)(2,1)}, u32[]{:S(2)}, u32[]{:S(2)}) %all-to-all-start) | async-done | bytes 8388640 | tf_op jit(solution)/shard_map/all_to_all | solution.py:60
  592.8 11.5 %convert_multiply_fusion = f32[128,32,1024]{2,0,1:T(8,128)} fusion(bf16[128,32,1024]{2,0,1:T(8,128)(2,1)} %all-to-all-done), kind=kLoop, calls=%fused_computation.11 | loop fusion | flops 8388608 | bytes 25165824 | tf_op jit(solution)/shard_map/mul | solution.py:35
  604.3 16.5 %fusion.2 = f32[4096,1024]{1,0:T(8,128)} fusion(f32[128,32,1024]{2,0,1:T(8,128)} %convert_multiply_fusion, f32[1024]{0:T(1024)S(1)} %get-tuple-element.37, f32[4096]{0:T(1024)S(1)} %bitcast.83, f32[1024]{0:T(1024)S(1)} %get-tuple-element.36, f32[4096]{0:T(1024)S(1)} %bitcast.81, f32[4096]{0:T(1024)S(1)} %copy-done.3), kind=kLoop, calls=%fused_computation.4 | loop fusion | flops 50331648 | bytes 33611776 | tf_op jit(solution)/shard_map/exp | solution.py:38
  620.8 6.4 gather_fusion
  627.2 0.1 iota_reduce_fusion
  627.3 10.1 %select_select_fusion = s32[1024]{0:T(1024)S(1)} fusion(s32[1024]{0:T(1024)S(1)} %get-tuple-element.7, s32[]{:T(128)} %bitcast.20, s32[]{:T(128)} %bitcast.21, s32[]{:T(128)} %bitcast.22, s32[]{:T(128)} %bitcast.23, s32[]{:T(128)} %bitcast.24, s32[]{:T(128)} %bitcast.25, s32[]{:T(128)} %bitcast.26, s32[]{:T(128)} %bitcast.27, s32[]{:T(128)} %bitcast.28, ...), kind=kLoop, calls=%fused_computation.51 | loop fusion | flops 37888 | bytes 8256 | tf_op jit(solution)/shard_map/jit(_take)/select_n | solution.py:41
  637.5 13.3 %fusion.7 = f32[1024]{0:T(1024)S(1)} fusion(f32[1024]{0:T(1024)S(1)} %get-tuple-element.37, f32[32,128]{1,0:T(8,128)S(1)} %bitcast.84, f32[1024]{0:T(1024)S(1)} %get-tuple-element.36, f32[32,128]{1,0:T(8,128)S(1)} %bitcast.82, f32[32,128]{1,0:T(8,128)S(1)} %bitcast.85, s32[1024]{0:T(1024)S(1)} %select_select_fusion, s32[32,128]{1,0:T(8,128)S(1)} %multiply_add_fusion, ...), kind=kLoop, calls=%fused_computation.10 | loop fusion | flops 71302144 | bytes 8470528 | tf_op jit(solution)/shard_map/reduce_sum | solution.py:43
  650.8 1.2 fusion.45
  652.7 11.9 %psum.7 = f32[1]{0:T(128)} all-reduce(f32[1]{0:T(128)} %bitcast.41), channel_id=1, replica_groups=mesh['site'=32,'band'=4] {'band'}, use_global_device_ids=true, to_apply=%region_3.4 | all-reduce | flops 1 | bytes 8 | tf_op jit(solution)/shard_map/psum | solution.py:83
  (17 shorter events, 0.1 us)
Async XLA Ops:
  0.6 16.0 %copy-start.4 = (s32[1,3]{1,0:T(1,128)S(1)}, s32[1,3]{1,0:T(1,128)}, u32[]{:S(2)}) copy-start(s32[1,3]{1,0:T(1,128)} %param.8) | copy-start | bytes 40
  0.6 16.7 %copy-start = (bf16[128,4,128]{2,1,0:T(4,128)(2,1)S(1)}, bf16[128,4,128]{2,1,0:T(4,128)(2,1)}, u32[]{:S(2)}) copy-start(bf16[128,4,128]{2,1,0:T(4,128)(2,1)} %param.7) | copy-start | bytes 393220
  12.0 185.4 %collective-permute-start.1 = (bf16[128,32,1024]{2,0,1:T(8,128)(2,1)}, bf16[128,32,1024]{2,0,1:T(8,128)(2,1)S(1)}, u32[]{:S(2)}, u32[]{:S(2)}) collective-permute-start(bf16[128,32,1024]{2,0,1:T(8,128)(2,1)} %copy.17), channel_id=1, source_target_pairs={{0,8},{4,12},{8,16},{12,20},{16,24},{20,28},{24,32},{28,36},{32,40... | collective-permute-start | bytes 25165832 | tf_op jit(solution)/shard_map/ppermute | solution.py:16
  13.3 361.6 %collective-permute-start = (bf16[128,32,1024]{2,0,1:T(8,128)(2,1)}, bf16[128,32,1024]{2,0,1:T(8,128)(2,1)S(1)}, u32[]{:S(2)}, u32[]{:S(2)}) collective-permute-start(bf16[128,32,1024]{2,0,1:T(8,128)(2,1)} %copy.17), channel_id=1, source_target_pairs={{0,4},{4,8},{8,12},{12,16},{16,20},{20,24},{24,28},{28,32},{32,36}... | collective-permute-start | bytes 25165832 | tf_op jit(solution)/shard_map/ppermute | solution.py:16
  15.2 368.4 %collective-permute-start.2 = (bf16[128,32,1024]{2,0,1:T(8,128)(2,1)}, bf16[128,32,1024]{2,0,1:T(8,128)(2,1)}, u32[]{:S(2)}, u32[]{:S(2)}) collective-permute-start(bf16[128,32,1024]{2,0,1:T(8,128)(2,1)} %copy.17), channel_id=1, source_target_pairs={{0,12},{4,16},{8,20},{12,24},{16,28},{20,32},{24,36},{28,40},{32,4... | collective-permute-start | bytes 25165832 | tf_op jit(solution)/shard_map/ppermute | solution.py:16
  407.2 89.8 %copy-start.1 = (s32[1,16]{1,0:T(1,128)S(1)}, s32[1,16]{1,0:T(1,128)}, u32[]{:S(2)}) copy-start(s32[1,16]{1,0:T(1,128)} %param.11) | copy-start | bytes 196
  407.2 90.6 %copy-start.2 = (f32[2,4096]{1,0:T(2,128)S(1)}, f32[2,4096]{1,0:T(2,128)}, u32[]{:S(2)}) copy-start(f32[2,4096]{1,0:T(2,128)} %param.10) | copy-start | bytes 98308
  407.2 185.6 %all-to-all-start = ((bf16[128,32,1024]{2,0,1:T(8,128)(2,1)}), bf16[128,32,1024]{2,0,1:T(8,128)(2,1)}, u32[]{:S(2)}, u32[]{:S(2)}) async-start(bf16[128,32,1024]{2,0,1:T(8,128)(2,1)} %add_convert_fusion), calls=%async_computation | async-start | bytes 16777216 | tf_op jit(solution)/shard_map/all_to_all | solution.py:60
  497.0 107.3 %copy-start.3 = (f32[4096]{0:T(1024)S(1)}, f32[4096]{0:T(1024)}, u32[]{:S(2)}) copy-start(f32[4096]{0:T(1024)} %param.9) | copy-start | bytes 49156
where the time goes:
time: 677 us; the launch traced here: 665 us
  waiting for transfers between devices  424 us (63%)
  starting transfers between devices  94.4 us (14%)
  matrix products  60.9 us (9%)
  other arithmetic  52.9 us (8%)
  local copies, waits for them, and re-layouts  19.2 us (3%)
  blocking collectives  11.9 us (2%)
    ppermute x3, waiting for transfers between devices, shifted(): return lax.ppermute(block, axis, route)  329 us
    all_to_all x1, waiting for transfers between devices, shards(): lax.all_to_all(total.astype(jnp.bfloat16), 'site', split_axis=1, concat_a...  94.9 us
    all_to_all x1, starting transfers between devices, shards(): lax.all_to_all(total.astype(jnp.bfloat16), 'site', split_axis=1, concat_a...  89.8 us
    dot_general x3, matrix products, shards(): jnp.einsum('ik,ktp->itp', weights, earlier, preferred_element_type=jnp.fl...  41.3 us
    dot_general x1, matrix products, shards(): jnp.einsum('ik,ktp->itp', factor[:, 0, :] * lower, fields, preferred_elem...  19.7 us
    exp x1, other arithmetic, coverage(): power = jnp.exp(ln_tenth * level)  16.5 us
  transfers between devices with their start and end apart: 4, of which 3 were waited for; matrix products, arithmetic and copies ran while one was open for 6% of the time, Pallas kernels for 0%

commit v1 on v0

v1 whole, which is shorter than its diff:
```python
import functools
import math

import jax
import jax.numpy as jnp
from jax import lax
from jax.experimental import pallas as pl
from jax.experimental.pallas import tpu as pltpu
from jax.sharding import PartitionSpec as P

MESH = pl.DeviceIdType.MESH
COLS = 256
SPACING = 0.03
CUTS = 4
PARTS = 2 * CUTS
BLOCK = 128
HALO = 3
ROW = 8
DB = math.log2(10.0) / 10.0
FIELD_GAIN = 8.0 * DB
NOTHING = -1e30
PEERS = ((0, 1), (1, 0), (3, 0), (1, 1), (3, 1), (2, 0), (2, 1))


def kernel(
    fields, weights, cand, tx, pos,
    best_out, sinr_out, mean_out,
    land, halo, mixed_in, loss, cand_loss, wbuf, site_x, site_y, site_a, cbuf,
    acc, tot, zred, msg, rows, msum, means,
    send_sem, recv_sem, zs, zr, w_send, w_recv, w2_send, w2_recv, c_send, c_recv,
    t_send, t_recv, o_send, o_recv, m_send, m_recv,
):
    site = lax.axis_index("site")
    band = lax.axis_index("band")
    z = site // 8
    j = site % 8
    x = j // 2
    c = j % 2
    cut = BLOCK // CUTS

    def at_row(dx, dc):
        return ((x + dx) % 4) * 2 + (c + dc) % 2

    barrier = pltpu.get_barrier_semaphore()
    count = 0
    for dx, dc in PEERS:
        pl.semaphore_signal(barrier, inc=1, device_id=(z * 8 + at_row(dx, dc), band), device_id_type=MESH)
        count += 1
    for dz in (1, 2, 3):
        pl.semaphore_signal(barrier, inc=1, device_id=(((z + dz) % 4) * 8 + j, band), device_id_type=MESH)
        count += 1
    for dy in (1, 2, 3):
        for dc in (0, 1):
            pl.semaphore_signal(
                barrier, inc=1, device_id=(z * 8 + at_row(0, dc), (band + dy) % 4), device_id_type=MESH
            )
            count += 1
    pl.semaphore_wait(barrier, count)

    def remote(src, dst, send, recv, to_site, to_band):
        return pltpu.make_async_remote_copy(
            src_ref=src, dst_ref=dst, send_sem=send, recv_sem=recv,
            device_id=(to_site, to_band), device_id_type=MESH,
        )

    quarter = pl.ds(pl.multiple_of(band * 32, 32), 32)

    def w_copy(dx):
        return remote(
            weights.at[quarter], wbuf.at[c, x, quarter], w_send.at[dx], w_recv.at[x],
            z * 8 + at_row(dx, 0), band,
        )

    def w2_copy(dc, dy):
        mine = wbuf.at[c, :, quarter]
        return remote(
            mine, mine, w2_send.at[dc * 4 + dy], w2_recv.at[c * 4 + band],
            z * 8 + at_row(0, dc), (band + dy) % 4,
        )

    def c_copy(q):
        dx, dc = PEERS[q]
        return remote(cand, cbuf.at[j], c_send.at[q], c_recv.at[j], z * 8 + at_row(dx, dc), band)

    w_own = pltpu.make_async_copy(weights.at[quarter], wbuf.at[c, x, quarter], w_recv.at[x])
    w_own.start()
    c_own = pltpu.make_async_copy(cand, cbuf.at[j], c_recv.at[j])
    c_own.start()
    for dx in (1, 2, 3):
        w_copy(dx).start()
    for q in range(7):
        c_copy(q).start()

    def piece(p):
        return pl.ds((p % CUTS) * cut, cut), pl.ds((p // CUTS) * 16, 16)

    def chunk(owner, p):
        sites, tiles = piece(p)
        return fields.at[sites, tiles, pl.ds(pl.multiple_of(owner * 128, 128), 128)]

    def landed(block, p):
        sites, tiles = piece(p)
        return land.at[block, sites, tiles]

    def send(q, p):
        dx, dc = PEERS[q]
        owner = at_row(dx, dc)
        return remote(
            chunk(owner, p), landed(j, p), send_sem.at[q * PARTS + p], recv_sem.at[j * PARTS + p],
            z * 8 + owner, band,
        )

    def forward(h, p):
        sites, tiles = piece(p)
        return remote(
            landed(ROW - HALO + h, p), halo.at[h, sites, tiles], zs.at[h * PARTS + p], zr.at[h * PARTS + p],
            ((z + 1) % 4) * 8 + j, band,
        )

    for p in range(PARTS):
        pltpu.make_async_copy(chunk(j, p), landed(j, p), recv_sem.at[j * PARTS + p]).start()
    for p in range(PARTS):
        for q in range(7):
            send(q, p).start()

    def arrived(block, p):
        ref = landed(block, p)
        pltpu.make_async_copy(ref, ref, recv_sem.at[block * PARTS + p]).wait()

    eight = pl.ds(pl.multiple_of(z * 8, 8), 8)
    xs_rows = pos[0, eight, :] * (8.0 * COLS * SPACING)
    ys_rows = pos[1, eight, :] * (4.0 * COLS * SPACING)
    tx_rows = (tx[eight, :] - 10.0) * DB
    for b in range(ROW):
        for ref, values in ((site_x, xs_rows), (site_y, ys_rows), (site_a, tx_rows)):
            ref[b] = jnp.transpose(jnp.broadcast_to(values[b : b + 1, :], (BLOCK, BLOCK)))

    lane = lax.broadcasted_iota(jnp.int32, (1, 128), 1)
    column = (j % 2) * 128 + lane
    pixel_row = band * 4 + j // 2

    def path_loss(b):
        @pl.loop(0, 16)
        def _(pair):
            for u in range(2):
                tile = pair * 2 + u
                px = ((tile % 8) * COLS + column).astype(jnp.float32) * SPACING
                py = ((tile // 8) * COLS + pixel_row).astype(jnp.float32) * SPACING
                dx = site_x[b] - px
                dy = site_y[b] - py
                d2 = dx * dx + dy * dy + SPACING * SPACING
                loss[pair, b * BLOCK : (b + 1) * BLOCK, u * 128 : (u + 1) * 128] = (
                    site_a[b] - (1.1 / math.log(2.0)) * jnp.log(d2)
                )

    def split_candidates():
        for b in range(ROW):
            ids = jnp.broadcast_to(cbuf[b, 0:1, :], (BLOCK, BLOCK))
            place = lax.broadcasted_iota(jnp.int32, (BLOCK, BLOCK), 0).astype(jnp.float32)
            hit = jnp.max(jnp.where(ids == place, 1.0, 0.0), axis=1, keepdims=True)
            is_cand = jnp.broadcast_to(hit, (BLOCK, BLOCK)) > 0.5
            where = (z * 4 + b // 2, slice(b * BLOCK, (b + 1) * BLOCK), slice((b % 2) * 128, (b % 2) * 128 + 128))
            level = loss[where]
            cand_loss[b] = jnp.where(is_cand, level, NOTHING)
            loss[where] = jnp.where(is_cand, NOTHING, level)

    def turn(source, block, p, row):
        first, half = (p % CUTS) * cut, p // CUTS
        values = source[block, first : first + cut, half * 16 : half * 16 + 16, :].astype(jnp.float32)
        turned = jnp.transpose(values, (1, 0, 2)).astype(jnp.bfloat16)
        for t in range(16):
            mixed_in[
                half * 8 + t // 2,
                pl.ds(pl.multiple_of(row * BLOCK + first, cut), cut),
                (t % 2) * 128 : (t % 2) * 128 + 128,
            ] = turned[t]

    def mix(half, b):
        w = wbuf[b % 2, b // 2]

        @pl.loop(0, 8)
        def _(step):
            pair = half * 8 + step
            fresh = mixed_in[pair, b * BLOCK : (b + 4) * BLOCK, :]
            mixed = jnp.dot(w, fresh, preferred_element_type=jnp.float32)
            power = jnp.exp2(loss[pair, b * BLOCK : (b + 1) * BLOCK, :] + FIELD_GAIN * mixed)
            acc[pair] += jnp.sum(power.reshape(BLOCK // 8, 8, 256), axis=0)

    acc[...] = jnp.zeros_like(acc)

    @pl.when(z == 0)
    def _():
        mixed_in[:, 0 : HALO * BLOCK, :] = jnp.zeros((16, HALO * BLOCK, 256), jnp.bfloat16)

    def halo_in(p):
        @pl.when(z > 0)
        def _():
            for h in range(HALO):
                forward(h, p).wait_recv()
                turn(halo, h, p, h)

    for p in range(PARTS):
        for h in (1, 2, 0):
            arrived(ROW - HALO + h, p)

            @pl.when(z < 3)
            def _():
                forward(h, p).start()

        if p < 4:
            path_loss(2 * p)
            path_loss(2 * p + 1)
        if p == 0:
            for dx in (1, 2, 3):
                other = (x + dx) % 4
                got = wbuf.at[c, other, quarter]
                pltpu.make_async_copy(got, got, w_recv.at[other]).wait()
            w_own.wait()
            for dc in (0, 1):
                for dy in range(4):
                    if dc or dy:
                        w2_copy(dc, dy).start()
        if p == 1:
            for b in range(ROW):
                pltpu.make_async_copy(cbuf.at[b], cbuf.at[b], c_recv.at[b]).wait()
            for dc in (0, 1):
                for dy in range(4):
                    if dc or dy:
                        other_c, other_y = (c + dc) % 2, (band + dy) % 4
                        got = wbuf.at[other_c, :, pl.ds(pl.multiple_of(other_y * 32, 32), 32)]
                        pltpu.make_async_copy(got, got, w2_recv.at[other_c * 4 + other_y]).wait()
        if p == 3:
            split_candidates()
        for b in range(ROW):
            if b < ROW - HALO:
                arrived(b, p)
            turn(land, b, p, b + HALO)
        if p == CUTS - 1:
            for b in range(HALO, ROW):
                mix(0, b)
        if p == CUTS + 1:
            for k in range(CUTS):
                halo_in(k)
        if p == CUTS + 2:
            for b in range(HALO):
                mix(0, b)
    for b in range(HALO, ROW):
        mix(1, b)
    for k in range(CUTS):
        halo_in(CUTS + k)
    for b in range(HALO):
        mix(1, b)

    for pair in range(16):
        both = jnp.sum(acc[pair], axis=0, keepdims=True)
        tot[2 * pair : 2 * pair + 1, :] = both[:, :128]
        tot[2 * pair + 1 : 2 * pair + 2, :] = both[:, 128:]

    def t_copy(dz):
        to = (z + dz) % 4
        return remote(
            tot.at[pl.ds(pl.multiple_of(to * 8, 8), 8)], zred.at[z], t_send.at[dz], t_recv.at[z], to * 8 + j, band
        )

    for dz in (1, 2, 3):
        t_copy(dz).start()

    bests, rests = [], []
    for b in range(ROW):
        lanes = slice((b % 2) * 128, (b % 2) * 128 + 128)
        fresh = mixed_in[z * 4 + b // 2, b * BLOCK : (b + 4) * BLOCK, lanes]
        mixed = jnp.dot(wbuf[b % 2, b // 2], fresh, preferred_element_type=jnp.float32)
        level = cand_loss[b]
        power = jnp.exp2(level + FIELD_GAIN * mixed)
        best = jnp.max(power, axis=0, keepdims=True)
        serves = (power == best) & (level > 0.5 * NOTHING)
        ties = jnp.sum(jnp.where(serves, 1.0, 0.0), axis=0, keepdims=True)
        rest = jnp.sum(jnp.where(serves, 0.0, power), axis=0, keepdims=True)
        bests.append(best)
        rests.append(rest + jnp.where(ties > 1.5, (ties - 1.0) * best, 0.0))
    best = jnp.concatenate(bests, axis=0)
    others = jnp.concatenate(rests, axis=0) + tot[eight, :]
    for dz in (1, 2, 3):
        came = (z + dz) % 4
        pltpu.make_async_copy(zred.at[came], zred.at[came], t_recv.at[came]).wait()
        others = others + zred[came]
    to_log10 = 1.0 / math.log(10.0)
    best_level = jnp.log(best) * to_log10
    sinr_level = jnp.log(best / others) * to_log10
    for b in range(ROW):
        msg[b, 0:1, :] = best_level[b : b + 1, :]
        msg[b, 1:2, :] = sinr_level[b : b + 1, :]

    def o_copy(q):
        owner = at_row(*PEERS[q])
        return remote(msg.at[owner], rows.at[j], o_send.at[q], o_recv.at[j], z * 8 + owner, band)

    for q in range(7):
        o_copy(q).start()
    rows[j] = msg[j]
    for q in range(7):
        came = at_row(*PEERS[q])
        pltpu.make_async_copy(rows.at[came], rows.at[came], o_recv.at[came]).wait()
    total = rows[0, 1:2, :]
    for k in range(1, ROW):
        total = total + rows[k, 1:2, :]
    msum[...] = jnp.broadcast_to(total, (8, 128))

    def m_copy(dy):
        return remote(msum, means.at[band], m_send.at[dy], m_recv.at[band], site, (band + dy) % 4)

    for dy in (1, 2, 3):
        m_copy(dy).start()
    means[band] = msum[...]
    for k in range(ROW):
        best_out[:, k * 128 : (k + 1) * 128] = rows[k, 0:1, :]
        sinr_out[:, k * 128 : (k + 1) * 128] = rows[k, 1:2, :]
    for dy in (1, 2, 3):
        came = (band + dy) % 4
        pltpu.make_async_copy(means.at[came], means.at[came], m_recv.at[came]).wait()
    total = (means[0] + means[1]) + (means[2] + means[3])
    mean = jnp.sum(total, axis=1, keepdims=True) * (1.0 / 4096.0)
    mean_out[...] = jnp.broadcast_to(mean, (8, 128))

    for q in range(7):
        c_copy(q).wait_send()
        o_copy(q).wait_send()
        for p in range(PARTS):
            send(q, p).wait_send()
    for dx in (1, 2, 3):
        w_copy(dx).wait_send()
        t_copy(dx).wait_send()
        m_copy(dx).wait_send()
    for dc in (0, 1):
        for dy in range(4):
            if dc or dy:
                w2_copy(dc, dy).wait_send()

    @pl.when(z < 3)
    def _():
        for h in range(HALO):
            for p in range(PARTS):
                forward(h, p).wait_send()


def shards(fields, factor, pattern, tx_power, site_position, candidates):
    block = fields.shape[0]
    lower = jnp.tril(jnp.ones((block, block), jnp.bfloat16))
    columns = [
        factor[:, d, :] * pattern[0, d - 1].astype(jnp.bfloat16) for d in (3, 2, 1)
    ] + [factor[:, 0, :] * lower]
    weights = jnp.concatenate(columns, axis=1)
    local = (candidates - lax.axis_index("site") * block).astype(jnp.float32)
    cand = jnp.broadcast_to(jnp.pad(local, ((0, 0), (0, 128 - local.shape[1])), constant_values=-1.0), (8, 128))
    dma = pltpu.SemaphoreType.DMA
    f32, bf16 = jnp.float32, jnp.bfloat16
    vmem = pl.BlockSpec(memory_space=pltpu.VMEM)
    best, sinr, mean = pl.pallas_call(
        kernel,
        out_shape=(
            jax.ShapeDtypeStruct((1, 1024), f32),
            jax.ShapeDtypeStruct((1, 1024), f32),
            jax.ShapeDtypeStruct((8, 128), f32),
        ),
        in_specs=[pl.BlockSpec(memory_space=pl.ANY), vmem, vmem, vmem, vmem],
        out_specs=(vmem, vmem, vmem),
        scratch_shapes=[
            pltpu.VMEM((ROW, BLOCK, 32, 128), bf16),
            pltpu.VMEM((HALO, BLOCK, 32, 128), bf16),
            pltpu.VMEM((16, (HALO + ROW) * BLOCK, 256), bf16),
            pltpu.VMEM((16, ROW * BLOCK, 256), f32),
            pltpu.VMEM((ROW, BLOCK, 128), f32),
            pltpu.VMEM((2, 4, BLOCK, 512), bf16),
            pltpu.VMEM((ROW, BLOCK, 128), f32),
            pltpu.VMEM((ROW, BLOCK, 128), f32),
            pltpu.VMEM((ROW, BLOCK, 128), f32),
            pltpu.VMEM((ROW, 8, 128), f32),
            pltpu.VMEM((16, 8, 256), f32),
            pltpu.VMEM((32, 128), f32),
            pltpu.VMEM((4, 8, 128), f32),
            pltpu.VMEM((ROW, 8, 128), f32),
            pltpu.VMEM((ROW, 8, 128), f32),
            pltpu.VMEM((8, 128), f32),
            pltpu.VMEM((4, 8, 128), f32),
            dma((7 * PARTS,)), dma((8 * PARTS,)), dma((HALO * PARTS,)), dma((HALO * PARTS,)),
            dma((4,)), dma((4,)), dma((8,)), dma((8,)), dma((7,)), dma((8,)),
            dma((4,)), dma((4,)), dma((7,)), dma((8,)), dma((4,)), dma((4,)),
        ],
        compiler_params=pltpu.CompilerParams(
            collective_id=0, has_side_effects=True, vmem_limit_bytes=56 << 20
        ),
    )(fields, weights, cand, tx_power.reshape(32, 128), site_position.reshape(2, 32, 128))
    return (best, sinr, mean[0, 0:1])


def solution(mesh):
    placed = (
        P("site", None, "band"),
        P("site", None, None),
        P("site", None),
        P(),
        P(),
        P("site", None),
    )
    return jax.shard_map(
        shards,
        mesh=mesh,
        in_specs=placed,
        out_specs=(P("site", "band"), P("site", "band"), P("site")),
        check_vma=False,
    )
```

time: 677 us -> 142 us (0.21)
  the two profiles are of different devices: /device:TPU:102 before, /device:TPU:1 now
where the time goes in v1:
time: 142 us
  Pallas kernels  129 us (91%)
  local copies, waits for them, and re-layouts  7.66 us (5%)
  other arithmetic  3.96 us (3%)
    pallas_call x1, Pallas kernels, shards(): pl.pallas_call(kernel, out_shape=(jax.ShapeDtypeStruct((1, 1024), f32), j...  129 us
    unnamed x3, local copies, waits for them, and re-layouts  3.9 us

profile of v1, /device:TPU:1, one launch (start us, length us, event | category | flops | bytes accessed | tf_op | source)
XLA Modules:
  0.0 141.8 jit_solution(5594529162965667324)
XLA Ops:
  0.6 1.4 fusion.5
  2.0 0.7 convert.5
  2.7 0.6 fusion.6
  3.3 1.3 fusion.2
  4.6 0.7 fusion.4
  5.3 0.7 pad_maximum_fusion.weights
  5.9 0.7 subtract_convert_fusion
  6.6 0.6 broadcast_in_dim.17.cand
  7.2 1.4 copy.31
  8.6 129.5 %shard_map.85 = (f32[1,1024]{1,0:T(1,128)}, f32[1,1024]{1,0:T(1,128)}, f32[8,128]{1,0:T(8,128)}) custom-call(bf16[128,32,1024]{2,1,0:T(8,128)(2,1)} %fields.1, bf16[128,512]{1,0:T(8,128)(2,1)} %pad_maximum_fusion.weights, f32[8,128]{1,0:T(8,128)} %broadcast_in_dim.17.cand, f32[32,128]{1,0:T(8,128)} %bitcast.23, f32[2,32,128]{2,1,0:T(8,128)} %bitcast.21), custom_call_target="tpu_custom_call" | custom-call | tf_op jit(solution)/shard_map/pallas_call | solution.py:358
  138.1 1.2 slice.34
  139.2 1.3 copy.34
  140.5 1.3 copy.35
  (2 shorter events, 0.0 us)

commit v2 on v1

v2 whole, which is shorter than its diff:
```python
import functools
import math

import jax
import jax.numpy as jnp
from jax import lax
from jax.experimental import pallas as pl
from jax.experimental.pallas import tpu as pltpu
from jax.sharding import PartitionSpec as P

MESH = pl.DeviceIdType.MESH
COLS = 256
SPACING = 0.03
PIECES = (
    (0, 0, 32), (0, 32, 32), (0, 64, 64),
    (1, 0, 32), (1, 32, 32), (1, 64, 32), (1, 96, 16), (1, 112, 16),
)
PARTS = len(PIECES)
HELD = 2
BLOCK = 128
HALO = 3
ROW = 8
DB = math.log2(10.0) / 10.0
FIELD_GAIN = 8.0 * DB
NOTHING = -1e30
PEERS = ((0, 1), (1, 0), (3, 0), (1, 1), (3, 1), (2, 0), (2, 1))


def kernel(
    fields, factor, pattern, tx_power, site_position, candidates,
    out,
    factor_in, pattern_in, tx, pos, cand_in,
    land, halo, mixed_in, loss, cand_loss, wbuf, site_x, site_y, site_a, cbuf,
    acc, rows, msum, means,
    send_sem, recv_sem, zs, zr, w_send, w_recv, w2_send, w2_recv, c_send, c_recv,
    o_send, o_recv, m_send, m_recv, local,
):
    site = lax.axis_index("site")
    band = lax.axis_index("band")
    z = site // 8
    j = site % 8
    x = j // 2
    c = j % 2
    quarter = pl.ds(pl.multiple_of(band * 32, 32), 32)
    row_sites = pl.ds(pl.multiple_of(z * 1024, 1024), 1024)
    small = [
        pltpu.make_async_copy(factor.at[quarter], factor_in, local.at[0]),
        pltpu.make_async_copy(pattern, pattern_in, local.at[1]),
        pltpu.make_async_copy(tx_power.at[:, row_sites], tx, local.at[2]),
        pltpu.make_async_copy(site_position.at[:, row_sites], pos, local.at[3]),
        pltpu.make_async_copy(candidates, cand_in, local.at[4]),
    ]
    for copy in small:
        copy.start()

    def at_row(dx, dc):
        return ((x + dx) % 4) * 2 + (c + dc) % 2

    barrier = pltpu.get_barrier_semaphore()
    count = 0
    for dz in range(4):
        for dx, dc in PEERS + (((0, 0),) if dz else ()):
            to = ((z + dz) % 4) * 8 + at_row(dx, dc)
            pl.semaphore_signal(barrier, inc=1, device_id=(to, band), device_id_type=MESH)
            count += 1
    for dy in (1, 2, 3):
        for dc in (0, 1):
            pl.semaphore_signal(
                barrier, inc=1, device_id=(z * 8 + at_row(0, dc), (band + dy) % 4), device_id_type=MESH
            )
            count += 1
    pl.semaphore_wait(barrier, count)

    def remote(src, dst, send, recv, to_site, to_band):
        return pltpu.make_async_remote_copy(
            src_ref=src, dst_ref=dst, send_sem=send, recv_sem=recv,
            device_id=(to_site, to_band), device_id_type=MESH,
        )

    def w_copy(dx):
        mine = wbuf.at[c, x, quarter]
        return remote(mine, mine, w_send.at[dx], w_recv.at[x], z * 8 + at_row(dx, 0), band)

    def w2_copy(dc, dy):
        mine = wbuf.at[c, :, quarter]
        return remote(
            mine, mine, w2_send.at[dc * 4 + dy], w2_recv.at[c * 4 + band],
            z * 8 + at_row(0, dc), (band + dy) % 4,
        )

    def c_copy(q):
        dx, dc = PEERS[q]
        return remote(cbuf.at[j], cbuf.at[j], c_send.at[q], c_recv.at[j], z * 8 + at_row(dx, dc), band)

    def piece(p):
        half, first, count = PIECES[p]
        return pl.ds(first, count), pl.ds(half * 16, 16)

    def chunk(owner, p):
        sites, tiles = piece(p)
        return fields.at[sites, tiles, pl.ds(pl.multiple_of(owner * 128, 128), 128)]

    def landed(block, p):
        sites, tiles = piece(p)
        return land.at[block, sites, tiles]

    def send(q, p):
        dx, dc = PEERS[q]
        owner = at_row(dx, dc)
        return remote(
            chunk(owner, p), landed(j, p), send_sem.at[q * PARTS + p], recv_sem.at[j * PARTS + p],
            z * 8 + owner, band,
        )

    def forward(h, p):
        sites, tiles = piece(p)
        return remote(
            landed(ROW - HALO + h, p), halo.at[h, sites, tiles], zs.at[h * PARTS + p], zr.at[h * PARTS + p],
            ((z + 1) % 4) * 8 + j, band,
        )

    for p in range(PARTS):
        pltpu.make_async_copy(chunk(j, p), landed(j, p), recv_sem.at[j * PARTS + p]).start()
    for q in range(7):
        send(q, 0).start()
    for copy in small:
        copy.wait()
    site_row = lax.broadcasted_iota(jnp.int32, (32, BLOCK), 0) + band * 32
    site_column = lax.broadcasted_iota(jnp.int32, (32, BLOCK), 1)
    for d in range(4):
        rows_of = factor_in[:, d, :].astype(jnp.float32)
        if d == 0:
            kept = jnp.where(site_column <= site_row, rows_of, 0.0)
        else:
            present = pattern_in[0:1, d - 1 : d].astype(jnp.float32)
            kept = rows_of * jnp.broadcast_to(present, (32, BLOCK))
        wbuf[c, x, quarter, (3 - d) * BLOCK : (4 - d) * BLOCK] = kept.astype(jnp.bfloat16)
    cbuf[j] = jnp.full((8, 128), -1.0, jnp.float32)
    cbuf[j, 0:1, 0:16] = (cand_in[...] - site * BLOCK).astype(jnp.float32)
    for dx in (1, 2, 3):
        w_copy(dx).start()
    for q in range(7):
        c_copy(q).start()
    for p in range(1, PARTS - HELD):
        for q in range(7):
            send(q, p).start()
    if HELD:
        @pl.when(j >= ROW - HALO)
        def _():
            for p in range(PARTS - HELD, PARTS):
                for q in range(7):
                    send(q, p).start()

    def arrived(block, p):
        ref = landed(block, p)
        pltpu.make_async_copy(ref, ref, recv_sem.at[block * PARTS + p]).wait()

    eight = pl.ds(pl.multiple_of(z * 8, 8), 8)
    for b in range(ROW):
        block = slice(b * BLOCK, (b + 1) * BLOCK)
        xs = pos[0:1, block] * (8.0 * COLS * SPACING)
        ys = pos[1:2, block] * (4.0 * COLS * SPACING)
        level = (tx[0:1, block] - 10.0) * DB
        for ref, values in ((site_x, xs), (site_y, ys), (site_a, level)):
            ref[b] = jnp.transpose(jnp.broadcast_to(values, (BLOCK, BLOCK)))

    lane = lax.broadcasted_iota(jnp.int32, (1, 128), 1)
    column = (j % 2) * 128 + lane
    pixel_row = band * 4 + j // 2

    def path_loss(b):
        @pl.loop(0, 16)
        def _(pair):
            for u in range(2):
                tile = pair * 2 + u
                px = ((tile % 8) * COLS + column).astype(jnp.float32) * SPACING
                py = ((tile // 8) * COLS + pixel_row).astype(jnp.float32) * SPACING
                dx = site_x[b] - px
                dy = site_y[b] - py
                d2 = dx * dx + dy * dy + SPACING * SPACING
                loss[pair, b * BLOCK : (b + 1) * BLOCK, u * 128 : (u + 1) * 128] = (
                    site_a[b] - (1.1 / math.log(2.0)) * jnp.log(d2)
                )

    def split_candidates():
        for b in range(ROW):
            ids = jnp.broadcast_to(cbuf[b, 0:1, :], (BLOCK, BLOCK))
            place = lax.broadcasted_iota(jnp.int32, (BLOCK, BLOCK), 0).astype(jnp.float32)
            hit = jnp.max(jnp.where(ids == place, 1.0, 0.0), axis=1, keepdims=True)
            is_cand = jnp.broadcast_to(hit, (BLOCK, BLOCK)) > 0.5
            where = (z * 4 + b // 2, slice(b * BLOCK, (b + 1) * BLOCK), slice((b % 2) * 128, (b % 2) * 128 + 128))
            level = loss[where]
            cand_loss[b] = jnp.where(is_cand, level, NOTHING)
            loss[where] = jnp.where(is_cand, NOTHING, level)

    def turn(source, block, p, row):
        half, first, count = PIECES[p]
        values = source[block, first : first + count, half * 16 : half * 16 + 16, :].astype(jnp.float32)
        turned = jnp.transpose(values, (1, 0, 2)).astype(jnp.bfloat16)
        for t in range(16):
            mixed_in[
                half * 8 + t // 2,
                row * BLOCK + first : row * BLOCK + first + count,
                (t % 2) * 128 : (t % 2) * 128 + 128,
            ] = turned[t]

    def mix(half, b):
        w = wbuf[b % 2, b // 2]

        @pl.loop(0, 8, unroll=8)
        def _(step):
            pair = half * 8 + step
            fresh = mixed_in[pair, b * BLOCK : (b + 4) * BLOCK, :]
            mixed = jnp.dot(w, fresh, preferred_element_type=jnp.float32)
            power = jnp.exp2(loss[pair, b * BLOCK : (b + 1) * BLOCK, :] + FIELD_GAIN * mixed)
            added = jnp.sum(power.reshape(BLOCK // 8, 8, 256), axis=0)
            acc[2 * pair, 0] += added[:, :128]
            acc[2 * pair + 1, 0] += added[:, 128:]

    acc[...] = jnp.zeros_like(acc)

    @pl.when(z == 0)
    def _():
        mixed_in[:, 0 : HALO * BLOCK, :] = jnp.zeros((16, HALO * BLOCK, 256), jnp.bfloat16)

    def halo_in(p):
        @pl.when(z > 0)
        def _():
            for h in range(HALO):
                forward(h, p).wait_recv()
                turn(halo, h, p, h)

    first_half = [p for p in range(PARTS) if PIECES[p][0] == 0]
    second_half = [p for p in range(PARTS) if PIECES[p][0] == 1]
    loss_blocks = {p: [b for b in range(ROW) if b * 3 // ROW == p] for p in range(3)}

    def serve(blocks):
        for b in blocks:
            tile = z * 8 + b
            lanes = slice((b % 2) * 128, (b % 2) * 128 + 128)
            fresh = mixed_in[z * 4 + b // 2, b * BLOCK : (b + 4) * BLOCK, lanes]
            mixed = jnp.dot(wbuf[b % 2, b // 2], fresh, preferred_element_type=jnp.float32)
            level = cand_loss[b]
            power = jnp.exp2(level + FIELD_GAIN * mixed)
            best = jnp.max(power, axis=0, keepdims=True)
            serves = (power == best) & (level > 0.5 * NOTHING)
            ties = jnp.sum(jnp.where(serves, 1.0, 0.0), axis=0, keepdims=True)
            rest = jnp.sum(jnp.where(serves, 0.0, power), axis=0, keepdims=True)
            acc[tile, 0, 0:1, :] += rest + jnp.where(ties > 1.5, (ties - 1.0) * best, 0.0)
            acc[tile, 1, 0:1, :] = best

    def o_copy(to_z, q):
        owner = to_z * 8 + (at_row(*PEERS[q]) if q < 7 else j)
        return remote(
            acc.at[owner], rows.at[z, j], o_send.at[to_z * 8 + q], o_recv.at[z * 8 + j], owner, band
        )

    def hand_over(half):
        for q in range(8):
            for to_z in (2 * half, 2 * half + 1):
                if q < 7:
                    o_copy(to_z, q).start()
                else:
                    @pl.when(to_z != z)
                    def _():
                        o_copy(to_z, q).start()

    def sent(p):
        for q in range(7):
            send(q, p).wait_send()

    def forwarded(pieces):
        @pl.when(z < 3)
        def _():
            for p in pieces:
                for h in range(HALO):
                    forward(h, p).wait_send()

    for p in range(PARTS):
        for h in (1, 2, 0):
            arrived(ROW - HALO + h, p)

            @pl.when(z < 3)
            def _():
                forward(h, p).start()

        if HELD and p == PARTS - HELD - 1:
            @pl.when(j < ROW - HALO)
            def _():
                for k in range(PARTS - HELD, PARTS):
                    for q in range(7):
                        send(q, k).start()

        for b in loss_blocks.get(p, ()):
            path_loss(b)
        if p == 0:
            for dx in (1, 2, 3):
                other = (x + dx) % 4
                got = wbuf.at[c, other, quarter]
                pltpu.make_async_copy(got, got, w_recv.at[other]).wait()
            for dc in (0, 1):
                for dy in range(4):
                    if dc or dy:
                        w2_copy(dc, dy).start()
        if p == 1:
            for q in range(7):
                other = at_row(*PEERS[q])
                pltpu.make_async_copy(cbuf.at[other], cbuf.at[other], c_recv.at[other]).wait()
            for dc in (0, 1):
                for dy in range(4):
                    if dc or dy:
                        other_c, other_y = (c + dc) % 2, (band + dy) % 4
                        got = wbuf.at[other_c, :, pl.ds(pl.multiple_of(other_y * 32, 32), 32)]
                        pltpu.make_async_copy(got, got, w2_recv.at[other_c * 4 + other_y]).wait()
        if p == 2:
            split_candidates()
        for b in range(ROW):
            if b < ROW - HALO:
                arrived(b, p)
            turn(land, b, p, b + HALO)
        if p == first_half[-1]:
            for b in range(HALO, ROW):
                mix(0, b)
        if p == second_half[1]:
            for k in first_half:
                halo_in(k)
            for b in range(HALO):
                mix(0, b)

            @pl.when(z < 2)
            def _():
                serve(range(ROW))

            hand_over(0)
        if p >= 2:
            sent(p - 2)
    for k in second_half[:-1]:
        halo_in(k)
    for b in range(HALO, ROW):
        mix(1, b)

    @pl.when(z >= 2)
    def _():
        serve(range(HALO, ROW))

    sent(PARTS - 2)
    sent(PARTS - 1)
    forwarded(range(PARTS - 1))
    halo_in(second_half[-1])
    for b in range(HALO):
        mix(1, b)

    @pl.when(z >= 2)
    def _():
        serve(range(HALO))

    hand_over(1)
    rows[z, j] = acc[site]
    for dz in range(4):
        for q in range(8 if dz else 7):
            from_z = (z + dz) % 4
            from_j = at_row(*PEERS[q]) if q < 7 else j
            came = rows.at[from_z, from_j]
            pltpu.make_async_copy(came, came, o_recv.at[from_z * 8 + from_j]).wait()
    others = jnp.sum((rows[0, :, 0] + rows[1, :, 0]) + (rows[2, :, 0] + rows[3, :, 0]), axis=1)
    best = jnp.max(rows[z, :, 1], axis=1)
    to_log10 = 1.0 / math.log(10.0)
    best_level = jnp.log(best) * to_log10
    sinr_level = jnp.log(best / others) * to_log10
    total = jnp.sum(sinr_level, axis=0, keepdims=True)
    msum[...] = jnp.broadcast_to(total, (8, 128))

    def m_copy(dy):
        return remote(msum, means.at[band], m_send.at[dy], m_recv.at[band], site, (band + dy) % 4)

    for dy in (1, 2, 3):
        m_copy(dy).start()
    means[band] = msum[...]
    out[0:8, :] = best_level
    out[8:16, :] = sinr_level
    for dy in (1, 2, 3):
        came = (band + dy) % 4
        pltpu.make_async_copy(means.at[came], means.at[came], m_recv.at[came]).wait()
    total = (means[0] + means[1]) + (means[2] + means[3])
    mean = jnp.sum(total, axis=1, keepdims=True) * (1.0 / 4096.0)
    out[16:24, :] = jnp.broadcast_to(mean, (8, 128))

    forwarded(range(PARTS - 1, PARTS))
    for q in range(7):
        c_copy(q).wait_send()
    for to_z in range(4):
        for q in range(7):
            o_copy(to_z, q).wait_send()

        @pl.when(to_z != z)
        def _():
            o_copy(to_z, 7).wait_send()

    for dx in (1, 2, 3):
        w_copy(dx).wait_send()
        m_copy(dx).wait_send()
    for dc in (0, 1):
        for dy in range(4):
            if dc or dy:
                w2_copy(dc, dy).wait_send()


def hand_out(out, best, sinr, mean):
    for k in range(8):
        best[:, k * 128 : (k + 1) * 128] = out[k : k + 1, :]
        sinr[:, k * 128 : (k + 1) * 128] = out[8 + k : 9 + k, :]
    mean[...] = out[16:17, :]


def shards(fields, factor, pattern, tx_power, site_position, candidates):
    dma = pltpu.SemaphoreType.DMA
    f32, bf16 = jnp.float32, jnp.bfloat16
    vmem = pl.BlockSpec(memory_space=pltpu.VMEM)
    out = pl.pallas_call(
        kernel,
        out_shape=jax.ShapeDtypeStruct((24, 128), f32),
        in_specs=[pl.BlockSpec(memory_space=pl.ANY)] * 6,
        out_specs=vmem,
        scratch_shapes=[
            pltpu.VMEM((32, 4, BLOCK), bf16),
            pltpu.VMEM((1, 3), jnp.int32),
            pltpu.VMEM((1, 1024), f32),
            pltpu.VMEM((2, 1024), f32),
            pltpu.VMEM((1, 16), jnp.int32),
            pltpu.VMEM((ROW, BLOCK, 32, 128), bf16),
            pltpu.VMEM((HALO, BLOCK, 32, 128), bf16),
            pltpu.VMEM((16, (HALO + ROW) * BLOCK, 256), bf16),
            pltpu.VMEM((16, ROW * BLOCK, 256), f32),
            pltpu.VMEM((ROW, BLOCK, 128), f32),
            pltpu.VMEM((2, 4, BLOCK, 512), bf16),
            pltpu.VMEM((ROW, BLOCK, 128), f32),
            pltpu.VMEM((ROW, BLOCK, 128), f32),
            pltpu.VMEM((ROW, BLOCK, 128), f32),
            pltpu.VMEM((ROW, 8, 128), f32),
            pltpu.VMEM((32, 2, 8, 128), f32),
            pltpu.VMEM((4, ROW, 2, 8, 128), f32),
            pltpu.VMEM((8, 128), f32),
            pltpu.VMEM((4, 8, 128), f32),
            dma((7 * PARTS,)), dma((8 * PARTS,)), dma((HALO * PARTS,)), dma((HALO * PARTS,)),
            dma((4,)), dma((4,)), dma((8,)), dma((8,)), dma((7,)), dma((8,)),
            dma((32,)), dma((32,)), dma((4,)), dma((4,)), dma((5,)),
        ],
        compiler_params=pltpu.CompilerParams(
            collective_id=0, has_side_effects=True, vmem_limit_bytes=56 << 20
        ),
    )(fields, factor, pattern, tx_power.reshape(1, -1), site_position, candidates)
    best, sinr, mean = pl.pallas_call(
        hand_out,
        out_shape=(
            jax.ShapeDtypeStruct((1, 1024), f32),
            jax.ShapeDtypeStruct((1, 1024), f32),
            jax.ShapeDtypeStruct((1, 128), f32),
        ),
        in_specs=[vmem],
        out_specs=(vmem, vmem, vmem),
    )(out)
    return (best, sinr, mean[0, 0:1])


def solution(mesh):
    placed = (
        P("site", None, "band"),
        P("site", None, None),
        P("site", None),
        P(),
        P(),
        P("site", None),
    )
    return jax.shard_map(
        shards,
        mesh=mesh,
        in_specs=placed,
        out_specs=(P("site", "band"), P("site", "band"), P("site")),
        check_vma=False,
    )
```

time: 142 us -> 121 us (0.85)
  the two profiles are of different devices: /device:TPU:1 before, /device:TPU:102 now
where the time goes in v2:
time: 121 us
  Pallas kernels  121 us (100%)
    pallas_call x1, Pallas kernels, shards(): pl.pallas_call(kernel, out_shape=jax.ShapeDtypeStruct((24, 128), f32), in...  119 us

profile of v2, /device:TPU:102, one launch (start us, length us, event | category | flops | bytes accessed | tf_op | source)
XLA Modules:
  0.0 121.1 jit_solution(12738952203742078504)
XLA Ops:
  0.6 119.2 %shard_map.85.out = f32[24,128]{1,0:T(8,128)} custom-call(bf16[128,32,1024]{2,1,0:T(8,128)(2,1)} %fields.1, bf16[128,4,128]{2,1,0:T(4,128)(2,1)} %factor.1, s32[1,3]{1,0:T(1,128)} %pattern.1, f32[1,4096]{1,0:T(1,128)} %bitcast.3, f32[2,4096]{1,0:T(2,128)} %site_position.1, s32[1,16]{1,0:T(1,128)} %candidates.1), custom_call_target="tpu_custom_call" | custom-call | tf_op jit(solution)/shard_map/pallas_call | solution.py:419
  119.8 1.3 %shard_map.86 = (f32[1,1024]{1,0:T(1,128)}, f32[1,1024]{1,0:T(1,128)}, f32[1,128]{1,0:T(1,128)}) custom-call(f32[24,128]{1,0:T(8,128)} %shard_map.85.out), custom_call_target="tpu_custom_call" | custom-call | tf_op jit(solution)/shard_map/pallas_call | solution.py:452

commit v3 on v2

--- a/solution.py
+++ b/solution.py
@@ -11,12 +11,11 @@
 MESH = pl.DeviceIdType.MESH
 COLS = 256
 SPACING = 0.03
-PIECES = (
-    (0, 0, 32), (0, 32, 32), (0, 64, 64),
-    (1, 0, 32), (1, 32, 32), (1, 64, 32), (1, 96, 16), (1, 112, 16),
-)
+PIECES = ((0, 0, 32), (0, 32, 32), (0, 64, 64), (1, 0, 32), (1, 32, 32), (1, 64, 32), (1, 96, 16), (1, 112, 8), (1, 120, 8))
 PARTS = len(PIECES)
-HELD = 2
+HELD = 3
+HELD_TO = (0, 1, 2, 3, 4, 5, 6)
+TRIGGER = PARTS - HELD - 1
 BLOCK = 128
 HALO = 3
 ROW = 8
@@ -108,7 +107,7 @@
         dx, dc = PEERS[q]
         owner = at_row(dx, dc)
         return remote(
-            chunk(owner, p), landed(j, p), send_sem.at[q * PARTS + p], recv_sem.at[j * PARTS + p],
+            chunk(owner, p), landed(j, p), send_sem.at[p], recv_sem.at[j * PARTS + p],
             z * 8 + owner, band,
         )
 
@@ -145,10 +144,15 @@
         for q in range(7):
             send(q, p).start()
     if HELD:
+        for p in range(PARTS - HELD, PARTS):
+            for q in range(7):
+                if q not in HELD_TO:
+                    send(q, p).start()
+
         @pl.when(j >= ROW - HALO)
         def _():
             for p in range(PARTS - HELD, PARTS):
-                for q in range(7):
+                for q in HELD_TO:
                     send(q, p).start()
 
     def arrived(block, p):
@@ -195,6 +199,10 @@
 
     def turn(source, block, p, row):
         half, first, count = PIECES[p]
+        if count == 8:
+            if first % 16 == 0:
+                return
+            first, count = first - 8, 16
         values = source[block, first : first + count, half * 16 : half * 16 + 16, :].astype(jnp.float32)
         turned = jnp.transpose(values, (1, 0, 2)).astype(jnp.bfloat16)
         for t in range(16):
@@ -252,7 +260,7 @@
     def o_copy(to_z, q):
         owner = to_z * 8 + (at_row(*PEERS[q]) if q < 7 else j)
         return remote(
-            acc.at[owner], rows.at[z, j], o_send.at[to_z * 8 + q], o_recv.at[z * 8 + j], owner, band
+            acc.at[owner], rows.at[z, j], o_send.at[0], o_recv.at[0], owner, band
         )
 
     def hand_over(half):
@@ -266,8 +274,9 @@
                         o_copy(to_z, q).start()
 
     def sent(p):
-        for q in range(7):
-            send(q, p).wait_send()
+        sites, tiles = piece(p)
+        seven = land.at[pl.ds(0, 7), sites, tiles]
+        pltpu.make_async_copy(seven, seven, send_sem.at[p]).wait()
 
     def forwarded(pieces):
         @pl.when(z < 3)
@@ -276,7 +285,7 @@
                 for h in range(HALO):
                     forward(h, p).wait_send()
 
-    for p in range(PARTS):
+    def pass_on(p):
         for h in (1, 2, 0):
             arrived(ROW - HALO + h, p)
 
@@ -284,13 +293,15 @@
             def _():
                 forward(h, p).start()
 
-        if HELD and p == PARTS - HELD - 1:
+        if HELD and p == TRIGGER:
             @pl.when(j < ROW - HALO)
             def _():
                 for k in range(PARTS - HELD, PARTS):
-                    for q in range(7):
+                    for q in HELD_TO:
                         send(q, k).start()
 
+    for p in range(PARTS - HELD):
+        pass_on(p)
         for b in loss_blocks.get(p, ()):
             path_loss(b)
         if p == 0:
@@ -332,10 +343,33 @@
                 serve(range(ROW))
 
             hand_over(0)
+        if p == 3:
+            for q in range(7):
+                c_copy(q).wait_send()
+            for dx in (1, 2, 3):
+                w_copy(dx).wait_send()
+            for dc in (0, 1):
+                for dy in range(4):
+                    if dc or dy:
+                        w2_copy(dc, dy).wait_send()
         if p >= 2:
             sent(p - 2)
-    for k in second_half[:-1]:
-        halo_in(k)
+    held = range(PARTS - HELD, PARTS)
+    for p in held:
+        pass_on(p)
+        for b in range(ROW - HALO, ROW):
+            turn(land, b, p, b + HALO)
+    late = held if HELD else (PARTS - 2, PARTS - 1)
+    for k in second_half:
+        if k not in late:
+            halo_in(k)
+    for p in range(PARTS - HELD - 2, PARTS - HELD):
+        sent(p)
+    forwarded(range(PARTS - HELD))
+    for p in held:
+        for b in range(ROW - HALO):
+            arrived(b, p)
+            turn(land, b, p, b + HALO)
     for b in range(HALO, ROW):
         mix(1, b)
 
@@ -343,10 +377,11 @@
     def _():
         serve(range(HALO, ROW))
 
-    sent(PARTS - 2)
-    sent(PARTS - 1)
-    forwarded(range(PARTS - 1))
-    halo_in(second_half[-1])
+    for p in held:
+        sent(p)
+    forwarded(held)
+    for p in late:
+        halo_in(p)
     for b in range(HALO):
         mix(1, b)
 
@@ -355,13 +390,8 @@
         serve(range(HALO))
 
     hand_over(1)
-    rows[z, j] = acc[site]
-    for dz in range(4):
-        for q in range(8 if dz else 7):
-            from_z = (z + dz) % 4
-            from_j = at_row(*PEERS[q]) if q < 7 else j
-            came = rows.at[from_z, from_j]
-            pltpu.make_async_copy(came, came, o_recv.at[from_z * 8 + from_j]).wait()
+    pltpu.make_async_copy(acc.at[site], rows.at[z, j], o_recv.at[0]).start()
+    pltpu.make_async_copy(rows, rows, o_recv.at[0]).wait()
     others = jnp.sum((rows[0, :, 0] + rows[1, :, 0]) + (rows[2, :, 0] + rows[3, :, 0]), axis=1)
     best = jnp.max(rows[z, :, 1], axis=1)
     to_log10 = 1.0 / math.log(10.0)
@@ -385,24 +415,10 @@
     mean = jnp.sum(total, axis=1, keepdims=True) * (1.0 / 4096.0)
     out[16:24, :] = jnp.broadcast_to(mean, (8, 128))
 
-    forwarded(range(PARTS - 1, PARTS))
-    for q in range(7):
-        c_copy(q).wait_send()
-    for to_z in range(4):
-        for q in range(7):
-            o_copy(to_z, q).wait_send()
-
-        @pl.when(to_z != z)
-        def _():
-            o_copy(to_z, 7).wait_send()
-
+    handed = acc.at[pl.ds(0, 31)]
+    pltpu.make_async_copy(handed, handed, o_send.at[0]).wait()
     for dx in (1, 2, 3):
-        w_copy(dx).wait_send()
         m_copy(dx).wait_send()
-    for dc in (0, 1):
-        for dy in range(4):
-            if dc or dy:
-                w2_copy(dc, dy).wait_send()
 
 
 def hand_out(out, best, sinr, mean):
@@ -418,7 +434,7 @@
     vmem = pl.BlockSpec(memory_space=pltpu.VMEM)
     out = pl.pallas_call(
         kernel,
-        out_shape=jax.ShapeDtypeStruct((24, 128), f32),
+        out_shape=pltpu.VMEM((24, 128), f32),
         in_specs=[pl.BlockSpec(memory_space=pl.ANY)] * 6,
         out_specs=vmem,
         scratch_shapes=[
@@ -441,9 +457,9 @@
             pltpu.VMEM((4, ROW, 2, 8, 128), f32),
             pltpu.VMEM((8, 128), f32),
             pltpu.VMEM((4, 8, 128), f32),
-            dma((7 * PARTS,)), dma((8 * PARTS,)), dma((HALO * PARTS,)), dma((HALO * PARTS,)),
+            dma((PARTS,)), dma((8 * PARTS,)), dma((HALO * PARTS,)), dma((HALO * PARTS,)),
             dma((4,)), dma((4,)), dma((8,)), dma((8,)), dma((7,)), dma((8,)),
-            dma((32,)), dma((32,)), dma((4,)), dma((4,)), dma((5,)),
+            dma((1,)), dma((1,)), dma((4,)), dma((4,)), dma((5,)),
         ],
         compiler_params=pltpu.CompilerParams(
             collective_id=0, has_side_effects=True, vmem_limit_bytes=56 << 20

time: 121 us -> 120 us (level)
  Pallas kernels: 121 us -> 118 us
    pallas_call x1, Pallas kernels: 119 us -> 117 us  [shards(): pl.pallas_call(kernel, out_shape=pltpu.VMEM((24, 128), f32), in_specs=[pl...]
where the time goes in v3:
time: 120 us; the launch traced here: 119 us
  Pallas kernels  118 us (98%)
    pallas_call x1, Pallas kernels, shards(): pl.pallas_call(kernel, out_shape=pltpu.VMEM((24, 128), f32), in_specs=[pl...  117 us

profile of v3, /device:TPU:102, one launch (start us, length us, event | category | flops | bytes accessed | tf_op | source)
XLA Modules:
  0.0 119.4 jit_solution(529431585964071500)
XLA Ops:
  0.6 116.9 %shard_map.85.out = f32[24,128]{1,0:T(8,128)S(1)} custom-call(bf16[128,32,1024]{2,1,0:T(8,128)(2,1)} %fields.1, bf16[128,4,128]{2,1,0:T(4,128)(2,1)} %factor.1, s32[1,3]{1,0:T(1,128)} %pattern.1, f32[1,4096]{1,0:T(1,128)} %bitcast.3, f32[2,4096]{1,0:T(2,128)} %site_position.1, s32[1,16]{1,0:T(1,128)} %candidates.1), custom_call_target="tpu_custom_call" | custom-call | tf_op jit(solution)/shard_map/pallas_call | solution.py:435
  117.5 0.0 copy-start
  117.5 0.6 copy-done
  118.1 1.3 %shard_map.86 = (f32[1,1024]{1,0:T(1,128)}, f32[1,1024]{1,0:T(1,128)}, f32[1,128]{1,0:T(1,128)}) custom-call(f32[24,128]{1,0:T(8,128)} %copy-done), custom_call_target="tpu_custom_call" | custom-call | tf_op jit(solution)/shard_map/pallas_call | solution.py:468
Async XLA Ops:
  117.5 0.6 copy-start

commit v4 on v3

--- a/solution.py
+++ b/solution.py
@@ -243,8 +243,8 @@
     loss_blocks = {p: [b for b in range(ROW) if b * 3 // ROW == p] for p in range(3)}
 
     def serve(blocks):
+        found = []
         for b in blocks:
-            tile = z * 8 + b
             lanes = slice((b % 2) * 128, (b % 2) * 128 + 128)
             fresh = mixed_in[z * 4 + b // 2, b * BLOCK : (b + 4) * BLOCK, lanes]
             mixed = jnp.dot(wbuf[b % 2, b // 2], fresh, preferred_element_type=jnp.float32)
@@ -254,7 +254,9 @@
             serves = (power == best) & (level > 0.5 * NOTHING)
             ties = jnp.sum(jnp.where(serves, 1.0, 0.0), axis=0, keepdims=True)
             rest = jnp.sum(jnp.where(serves, 0.0, power), axis=0, keepdims=True)
-            acc[tile, 0, 0:1, :] += rest + jnp.where(ties > 1.5, (ties - 1.0) * best, 0.0)
+            found.append((z * 8 + b, best, rest + jnp.where(ties > 1.5, (ties - 1.0) * best, 0.0)))
+        for tile, best, rest in found:
+            acc[tile, 0, 0:1, :] += rest
             acc[tile, 1, 0:1, :] = best
 
     def o_copy(to_z, q):
@@ -377,9 +379,6 @@
     def _():
         serve(range(HALO, ROW))
 
-    for p in held:
-        sent(p)
-    forwarded(held)
     for p in late:
         halo_in(p)
     for b in range(HALO):
@@ -390,6 +389,9 @@
         serve(range(HALO))
 
     hand_over(1)
+    for p in held:
+        sent(p)
+    forwarded(held)
     pltpu.make_async_copy(acc.at[site], rows.at[z, j], o_recv.at[0]).start()
     pltpu.make_async_copy(rows, rows, o_recv.at[0]).wait()
     others = jnp.sum((rows[0, :, 0] + rows[1, :, 0]) + (rows[2, :, 0] + rows[3, :, 0]), axis=1)

time: 120 us -> 120 us (level)
  no operation moved by 1% of the time
where the time goes in v4:
time: 120 us
  Pallas kernels  119 us (99%)
    pallas_call x1, Pallas kernels, shards(): pl.pallas_call(kernel, out_shape=pltpu.VMEM((24, 128), f32), in_specs=[pl...  117 us

profile of v4, /device:TPU:102, one launch (start us, length us, event | category | flops | bytes accessed | tf_op | source)
XLA Modules:
  0.0 119.9 jit_solution(10911739006965512044)
XLA Ops:
  0.6 117.3 %shard_map.85.out = f32[24,128]{1,0:T(8,128)S(1)} custom-call(bf16[128,32,1024]{2,1,0:T(8,128)(2,1)} %fields.1, bf16[128,4,128]{2,1,0:T(4,128)(2,1)} %factor.1, s32[1,3]{1,0:T(1,128)} %pattern.1, f32[1,4096]{1,0:T(1,128)} %bitcast.3, f32[2,4096]{1,0:T(2,128)} %site_position.1, s32[1,16]{1,0:T(1,128)} %candidates.1), custom_call_target="tpu_custom_call" | custom-call | tf_op jit(solution)/shard_map/pallas_call | solution.py:437
  117.9 0.0 copy-start
  118.0 0.6 copy-done
  118.5 1.3 %shard_map.86 = (f32[1,1024]{1,0:T(1,128)}, f32[1,1024]{1,0:T(1,128)}, f32[1,128]{1,0:T(1,128)}) custom-call(f32[24,128]{1,0:T(8,128)} %copy-done), custom_call_target="tpu_custom_call" | custom-call | tf_op jit(solution)/shard_map/pallas_call | solution.py:470
Async XLA Ops:
  117.9 0.6 copy-start

commit v5 on v3

--- a/solution.py
+++ b/solution.py
@@ -149,7 +149,7 @@
                 if q not in HELD_TO:
                     send(q, p).start()
 
-        @pl.when(j >= ROW - HALO)
+        @pl.when(j >= 4)
         def _():
             for p in range(PARTS - HELD, PARTS):
                 for q in HELD_TO:
@@ -294,7 +294,7 @@
                 forward(h, p).start()
 
         if HELD and p == TRIGGER:
-            @pl.when(j < ROW - HALO)
+            @pl.when(j < 4)
             def _():
                 for k in range(PARTS - HELD, PARTS):
                     for q in HELD_TO:
@@ -367,10 +367,14 @@
         sent(p)
     forwarded(range(PARTS - HELD))
     for p in held:
-        for b in range(ROW - HALO):
+        arrived(4, p)
+        turn(land, 4, p, 4 + HALO)
+    mix(1, 7)
+    for p in held:
+        for b in range(4):
             arrived(b, p)
             turn(land, b, p, b + HALO)
-    for b in range(HALO, ROW):
+    for b in range(HALO, ROW - 1):
         mix(1, b)
 
     @pl.when(z >= 2)

time: 120 us -> 120 us (level)
  no operation moved by 1% of the time
where the time goes in v5:
time: 120 us
  Pallas kernels  119 us (99%)
    pallas_call x1, Pallas kernels, shards(): pl.pallas_call(kernel, out_shape=pltpu.VMEM((24, 128), f32), in_specs=[pl...  117 us

profile of v5, /device:TPU:102, one launch (start us, length us, event | category | flops | bytes accessed | tf_op | source)
XLA Modules:
  0.0 119.8 jit_solution(12232388357525402907)
XLA Ops:
  0.6 117.2 %shard_map.85.out = f32[24,128]{1,0:T(8,128)S(1)} custom-call(bf16[128,32,1024]{2,1,0:T(8,128)(2,1)} %fields.1, bf16[128,4,128]{2,1,0:T(4,128)(2,1)} %factor.1, s32[1,3]{1,0:T(1,128)} %pattern.1, f32[1,4096]{1,0:T(1,128)} %bitcast.3, f32[2,4096]{1,0:T(2,128)} %site_position.1, s32[1,16]{1,0:T(1,128)} %candidates.1), custom_call_target="tpu_custom_call" | custom-call | tf_op jit(solution)/shard_map/pallas_call | solution.py:439
  117.8 0.0 copy-start
  117.9 0.6 copy-done
  118.4 1.3 %shard_map.86 = (f32[1,1024]{1,0:T(1,128)}, f32[1,1024]{1,0:T(1,128)}, f32[1,128]{1,0:T(1,128)}) custom-call(f32[24,128]{1,0:T(8,128)} %copy-done), custom_call_target="tpu_custom_call" | custom-call | tf_op jit(solution)/shard_map/pallas_call | solution.py:472
Async XLA Ops:
  117.8 0.6 copy-start
